TPU v7x, 32 devices: a whole 2x2x4 slice. The times are simulated.
32 devices in a mesh: dp: 8 (over y, x, core), seq: 4 (over z).
Axes of the slice: x: 2, y: 2, z: 4, core: 2. Of those that a mesh axis runs over, the one named last changes fastest.
Arguments:
- queries: bfloat16 [8, 2048, 2048], P('dp', 'seq'), may hold values from -650 to 650
- keys_values: bfloat16 [8, 2048, 1024], P('dp', 'seq'), may hold values from -28 to 28
- doc_blocks: int32 [8, 16], P('dp'), may hold values from 0 to 3, never falling along the last dimension, each value on 1 to 8 neighbouring positions
- route_plan: int32 [4, 4], P('seq'), may hold values from 0 to 7, as said below
- out_weight: bfloat16 [2048, 4096], P('dp'), may hold values from -0.125 to 0.125
Outputs:
- layer_out: bfloat16 [8, 2048, 4096], P('dp', 'seq')
Inputs may be any that keep to these rules, and one draw needn't show every extreme that they name: Within a row of route_plan the entries are distinct.
All inputs are finite; a program needn't handle non-finite values.
Results may differ from a plain program's by a relative error of at most 0.0053.
Values may be sent and summed in bfloat16 or wider, within the bound.
A program may use at most 256 MiB of HBM per device.

v0:
```python
import math

import jax
import jax.numpy as jnp
from jax import lax
from jax.sharding import PartitionSpec as P

HEAD_DIM = 128
BLOCK = 128


neg_fill = -1e30


def swapped(block, axis, stride):
    count = lax.axis_size(axis)
    route = []
    for low in range(count):
        high = low | 1 << stride
        if high != low and high < count:
            route += [(low, high), (high, low)]
    return lax.ppermute(block, axis, route)


def attend_local(query_seq, pair_seq, doc_ids):
    seq_rows = query_seq.shape[0]
    local_heads = query_seq.shape[1] // HEAD_DIM
    local_pairs = pair_seq.shape[1] // (2 * HEAD_DIM)
    per_pair = local_heads // local_pairs
    query_view = query_seq.reshape(seq_rows, local_pairs, per_pair, HEAD_DIM)
    pair_view = pair_seq.reshape(seq_rows, local_pairs, 2, HEAD_DIM)
    key_view = pair_view[:, :, 0]
    value_view = pair_view[:, :, 1]
    token_doc = jnp.repeat(doc_ids, BLOCK)
    tile_rows = min(512, seq_rows)
    score_scale = 1.0 / math.sqrt(HEAD_DIM)

    def per_tile(tile_index):
        first_row = tile_index * tile_rows
        query_tile = lax.dynamic_slice_in_dim(query_view, first_row, tile_rows, 0)
        query_pos = first_row + jnp.arange(tile_rows, dtype=jnp.int32)
        query_doc = lax.dynamic_slice_in_dim(token_doc, first_row, tile_rows, 0)

        def key_step(key_index, running_state):
            row_max, totals, summed = running_state
            key_first = key_index * tile_rows
            key_tile = lax.dynamic_slice_in_dim(key_view, key_first, tile_rows, 0)
            value_tile = lax.dynamic_slice_in_dim(value_view, key_first, tile_rows, 0)
            key_doc = lax.dynamic_slice_in_dim(token_doc, key_first, tile_rows, 0)
            key_pos = key_first + jnp.arange(tile_rows, dtype=jnp.int32)
            scores = (
                jnp.einsum(
                    "qcgd,kcd->cgqk", query_tile, key_tile, preferred_element_type=jnp.float32
                )
                * score_scale
            )
            allowed = (query_doc[:, None] == key_doc[None, :]) & (
                key_pos[None, :] <= query_pos[:, None]
            )
            scores = jnp.where(allowed, scores, neg_fill)
            new_max = jnp.maximum(row_max, scores.max(-1))
            rescale = jnp.exp(row_max - new_max)
            weights = jnp.where(allowed, jnp.exp(scores - new_max[..., None]), 0.0)
            totals = totals * rescale + weights.sum(-1)
            rounded = weights.astype(jnp.bfloat16)
            product = jnp.einsum(
                "cgqk,kcd->qcgd", rounded, value_tile, preferred_element_type=jnp.float32
            )
            summed = summed * jnp.transpose(rescale, (2, 0, 1))[..., None] + product
            return (new_max, totals, summed)

        doc_start = jnp.sum((doc_ids[None, :] < doc_ids[:, None]).astype(jnp.int32), axis=1)
        lowest = doc_start[first_row // BLOCK] * BLOCK // tile_rows
        start_state = (
            jnp.full((local_pairs, per_pair, tile_rows), neg_fill, jnp.float32),
            jnp.zeros((local_pairs, per_pair, tile_rows), jnp.float32),
            jnp.zeros((tile_rows, local_pairs, per_pair, HEAD_DIM), jnp.float32),
        )
        row_max, totals, summed = lax.fori_loop(lowest, tile_index + 1, key_step, start_state)
        attended = summed / jnp.transpose(totals, (2, 0, 1))[..., None]
        return attended.astype(jnp.bfloat16).reshape(tile_rows, local_heads * HEAD_DIM)

    tile_out = lax.map(per_tile, jnp.arange(seq_rows // tile_rows, dtype=jnp.int32))
    return tile_out.reshape(seq_rows, local_heads * HEAD_DIM)


def swap_bit(query_rows, pair_rows, xor_marks, bit_index):
    partner_query, partner_pairs = swapped((query_rows, pair_rows), "dp", bit_index)
    moving = (jnp.right_shift(xor_marks, bit_index) % 2 == 1)[:, None, None]
    return (
        jnp.where(moving, partner_query, query_rows),
        jnp.where(moving, partner_pairs, pair_rows),
    )


def body(queries, keys_values, doc_blocks, route_plan, out_weight):
    rows_dev = queries.shape[1]
    query_width = queries.shape[2]
    pair_width = keys_values.shape[2]
    blocks = rows_dev // BLOCK
    query_rows = queries[0].reshape(blocks, BLOCK, query_width)
    pair_rows = keys_values[0].reshape(blocks, BLOCK, pair_width)
    xor_marks = route_plan[0]
    group_count = lax.axis_size("dp")
    bit_list = list(range(group_count.bit_length() - 1))
    for bit_index in bit_list:
        query_rows, pair_rows = swap_bit(query_rows, pair_rows, xor_marks, bit_index)
    seq_count = lax.axis_size("seq")
    query_tok = query_rows.reshape(rows_dev, query_width)
    pair_heads = pair_width // (2 * HEAD_DIM)
    repeats = max(1, seq_count // pair_heads)
    pair_wide = jnp.repeat(pair_rows.reshape(rows_dev, pair_heads, 2 * HEAD_DIM), repeats, axis=1)
    pair_wide = pair_wide.reshape(rows_dev, pair_heads * repeats * 2 * HEAD_DIM)
    query_seq, pair_seq = (
        lax.all_to_all(query_tok, "seq", split_axis=1, concat_axis=0, tiled=True),
        lax.all_to_all(pair_wide, "seq", split_axis=1, concat_axis=0, tiled=True),
    )
    attended = attend_local(query_seq, pair_seq, doc_blocks[0])
    attended_rows = lax.all_to_all(attended, "seq", split_axis=0, concat_axis=1, tiled=True)
    layer_out = jnp.dot(
        attended_rows,
        lax.all_gather(out_weight, "dp", axis=0, tiled=True),
        preferred_element_type=jnp.float32,
    )
    return layer_out.astype(jnp.bfloat16)[None]


def solution(mesh):
    in_specs = (
        P("dp", "seq", None),
        P("dp", "seq", None),
        P("dp", None),
        P("seq", None),
        P("dp", None),
    )
    out_specs = P("dp", "seq", None)
    return jax.shard_map(body, mesh=mesh, in_specs=in_specs, out_specs=out_specs, check_vma=False)
```

profile of v0, /device:TPU:0, one launch (start us, length us, event | category | flops | bytes accessed | tf_op | source)
XLA Modules:
  0.0 333.8 jit_solution(14645394502636633836)
XLA Ops:
  7.7 3.3 collective-permute-done
  11.0 2.0 broadcast_select_fusion
  12.9 2.9 collective-permute-start.1
  16.2 68.1 %collective-permute-done.4 = bf16[4,128,1024]{2,1,0:T(8,128)(2,1)S(1)} collective-permute-done((bf16[4,128,1024]{2,1,0:T(8,128)(2,1)S(1)}, bf16[4,128,1024]{2,1,0:T(8,128)(2,1)S(1)}, u32[]{:S(2)}, u32[]{:S(2)}) %collective-permute-start.4) | collective-permute-done | bytes 1048608 | tf_op jit(solution)/shard_map/ppermute | solution.py:22
  84.5 1.8 collective-permute-start.5
  86.9 23.7 %collective-permute-done.5 = bf16[4,128,1024]{2,1,0:T(8,128)(2,1)S(1)} collective-permute-done((bf16[4,128,1024]{2,1,0:T(8,128)(2,1)S(1)}, bf16[4,128,1024]{2,1,0:T(8,128)(2,1)S(1)}, u32[]{:S(2)}, u32[]{:S(2)}) %collective-permute-start.5) | collective-permute-done | bytes 1048608 | tf_op jit(solution)/shard_map/ppermute | solution.py:22
  111.7 2.6 all_to_all.39
  114.4 2.3 copy.27
  116.7 5.1 %all-to-all-start.1 = ((bf16[512,4,256]{2,0,1:T(8,128)(2,1)}), bf16[512,4,256]{2,0,1:T(8,128)(2,1)}, u32[]{:S(2)}, u32[]{:S(2)}) async-start(bf16[512,4,256]{2,0,1:T(8,128)(2,1)} %copy.27), calls=%async_computation.1 | async-start | bytes 2097152 | tf_op jit(solution)/shard_map/all_to_all | solution.py:116
  121.9 32.4 %collective-permute-done.2 = bf16[4,128,2048]{2,1,0:T(8,128)(2,1)} collective-permute-done((bf16[4,128,2048]{2,1,0:T(8,128)(2,1)S(1)}, bf16[4,128,2048]{2,1,0:T(8,128)(2,1)}, u32[]{:S(2)}, u32[]{:S(2)}) %collective-permute-start.2) | collective-permute-done | bytes 2097184 | tf_op jit(solution)/shard_map/ppermute | solution.py:22
  154.3 3.2 broadcast_select_fusion.2
  157.4 3.3 all_to_all.36
  160.8 1.7 copy.26
  162.5 4.8 %all-to-all-start = ((bf16[512,4,512]{2,0,1:T(8,128)(2,1)}), bf16[512,4,512]{2,0,1:T(8,128)(2,1)}, u32[]{:S(2)}, u32[]{:S(2)}) async-start(bf16[512,4,512]{2,0,1:T(8,128)(2,1)} %copy.26), calls=%async_computation | async-start | bytes 4194304 | tf_op jit(solution)/shard_map/all_to_all | solution.py:115
  168.1 1.3 reshape.131
  169.5 2.3 fusion.34
  171.8 2.3 copy.31
  174.2 40.2 %all-to-all-done = bf16[512,4,512]{2,0,1:T(8,128)(2,1)} async-done(((bf16[512,4,512]{2,0,1:T(8,128)(2,1)}), bf16[512,4,512]{2,0,1:T(8,128)(2,1)}, u32[]{:S(2)}, u32[]{:S(2)}) %all-to-all-start) | async-done | bytes 2097184 | tf_op jit(solution)/shard_map/all_to_all | solution.py:115
  214.4 4.0 %reshape.129 = bf16[2048,1,4,128]{3,2,0,1:T(4,128)(2,1)} reshape(bf16[4,512,512]{2,1,0:T(8,128)(2,1)} %bitcast.11) | data formatting | bytes 4194304 | tf_op jit(solution)/shard_map/reshape | solution.py:30
  218.4 47.3 %while.45 = (s32[]{:T(128)}, bf16[4,512,512]{1,2,0:T(8,128)(2,1)}, s32[1,16]{1,0:T(1,128)S(1)}, s32[4]{0:T(128)S(1)}, bf16[2048,1,4,128]{3,2,0,1:T(4,128)(2,1)},...) while((s32[]{:T(128)}, bf16[4,512,512]{1,2,0:T(8,128)(2,1)}, ...), condition=%wide.region_6.7_spmd, body=%wide.region_0.6_spmd.sunk | while | flops 552345344 | bytes 22460004 | solution.py:83
  223.2 4.0 %while.46 = (s32[]{:T(128)}, f32[1,4,512]{2,1,0:T(4,128)S(1)}, f32[1,4,512]{2,1,0:T(4,128)S(1)}, f32[512,1,4,128]{0,3,2,1:T(8,128)S(1)}, s32[]{:T(128)}, /*index...) while((s32[]{:T(128)}, f32[1,4,512]{2,1,0:T(4,128)S(1)}, ...), condition=%wide.region_5.5_spmd.clone, body=%wide.region_2.4_spmd.clone.sunk | while | flops 551820288 | bytes 16662735 | solution.py:79
  224.5 1.6 fusion.48
  233.0 8.0 %while.46 = (s32[]{:T(128)}, f32[1,4,512]{2,1,0:T(4,128)S(1)}, f32[1,4,512]{2,1,0:T(4,128)S(1)}, f32[512,1,4,128]{0,3,2,1:T(8,128)S(1)}, s32[]{:T(128)}, /*index...) while((s32[]{:T(128)}, f32[1,4,512]{2,1,0:T(4,128)S(1)}, ...), condition=%wide.region_5.5_spmd.clone, body=%wide.region_2.4_spmd.clone.sunk | while | flops 551820288 | bytes 16662735 | solution.py:79
  234.3 1.6 fusion.48
  238.3 1.6 fusion.48
  246.8 4.0 %while.46 = (s32[]{:T(128)}, f32[1,4,512]{2,1,0:T(4,128)S(1)}, f32[1,4,512]{2,1,0:T(4,128)S(1)}, f32[512,1,4,128]{0,3,2,1:T(8,128)S(1)}, s32[]{:T(128)}, /*index...) while((s32[]{:T(128)}, f32[1,4,512]{2,1,0:T(4,128)S(1)}, ...), condition=%wide.region_5.5_spmd.clone, body=%wide.region_2.4_spmd.clone.sunk | while | flops 551820288 | bytes 16662735 | solution.py:79
  248.1 1.6 fusion.48
  256.7 8.0 %while.46 = (s32[]{:T(128)}, f32[1,4,512]{2,1,0:T(4,128)S(1)}, f32[1,4,512]{2,1,0:T(4,128)S(1)}, f32[512,1,4,128]{0,3,2,1:T(8,128)S(1)}, s32[]{:T(128)}, /*index...) while((s32[]{:T(128)}, f32[1,4,512]{2,1,0:T(4,128)S(1)}, ...), condition=%wide.region_5.5_spmd.clone, body=%wide.region_2.4_spmd.clone.sunk | while | flops 551820288 | bytes 16662735 | solution.py:79
  258.0 1.6 fusion.48
  262.0 1.6 fusion.48
  265.6 47.4 %all_to_all.48 = bf16[4,512,512]{1,2,0:T(8,128)(2,1)S(1)} all-to-all(bf16[4,512,512]{1,2,0:T(8,128)(2,1)} %get-tuple-element.193), channel_id=1, replica_groups=mesh['dp'=8,'seq'=4] {'seq'}, dimensions={0} | all-to-all | bytes 4194304 | tf_op jit(solution)/shard_map/all_to_all | solution.py:119
  313.1 13.9 %fusion.27 = bf16[1,512,4096]{2,1,0:T(8,128)(2,1)} fusion(bf16[512,2048]{0,1:T(8,128)(2,1)S(1)} %bitcast.130, bf16[2048,4096]{1,0:T(8,128)(2,1)} %all-gather.2.cloned.1.call-done), kind=kOutput, calls=%fused_computation.34 | convolution fusion | flops 8592031744 | bytes 23068672 | tf_op jit(solution)/shard_map/dot_general | solution.py:120
  (115 shorter events, 33.4 us)
Async XLA Ops:
  6.5 4.5 %collective-permute-start = (bf16[4,128,2048]{2,1,0:T(8,128)(2,1)}, bf16[4,128,2048]{2,1,0:T(8,128)(2,1)S(1)}, u32[]{:S(2)}, u32[]{:S(2)}) collective-permute-start(bf16[4,128,2048]{2,1,0:T(8,128)(2,1)} %bitcast.128), channel_id=1, source_target_pairs={{0,4},{4,0},{8,12},{12,8},{16,20},{20,16},{24,28},{28,24},{1,5},{5... | collective-permute-start | bytes 6291464 | tf_op jit(solution)/shard_map/ppermute | solution.py:22
  7.0 8.9 %collective-permute-start.3 = (bf16[4,128,1024]{2,1,0:T(8,128)(2,1)}, bf16[4,128,1024]{2,1,0:T(8,128)(2,1)S(1)}, u32[]{:S(2)}, u32[]{:S(2)}) collective-permute-start(bf16[4,128,1024]{2,1,0:T(8,128)(2,1)} %bitcast.131), channel_id=1, source_target_pairs={{0,4},{4,0},{8,12},{12,8},{16,20},{20,16},{24,28},{28,24},{1,5},{5... | collective-permute-start | bytes 3145736 | tf_op jit(solution)/shard_map/ppermute | solution.py:22
  11.0 4.9 %copy-start = (bf16[1,512,1024]{2,1,0:T(8,128)(2,1)S(1)}, bf16[1,512,1024]{2,1,0:T(8,128)(2,1)}, u32[]{:S(2)}) copy-start(bf16[1,512,1024]{2,1,0:T(8,128)(2,1)} %param.10) | copy-start | bytes 3145732
  12.9 73.3 %collective-permute-start.1 = (bf16[4,128,2048]{2,1,0:T(8,128)(2,1)S(1)}, bf16[4,128,2048]{2,1,0:T(8,128)(2,1)S(1)}, u32[]{:S(2)}, u32[]{:S(2)}) collective-permute-start(bf16[4,128,2048]{2,1,0:T(8,128)(2,1)S(1)} %broadcast_select_fusion), channel_id=1, source_target_pairs={{0,8},{8,0},{4,12},{12,4},{16,24},{24,16},{20,28},{28,20},{1,9},{9... | collective-permute-start | bytes 6291464 | tf_op jit(solution)/shard_map/ppermute | solution.py:22
  16.1 68.2 %collective-permute-start.4 = (bf16[4,128,1024]{2,1,0:T(8,128)(2,1)S(1)}, bf16[4,128,1024]{2,1,0:T(8,128)(2,1)S(1)}, u32[]{:S(2)}, u32[]{:S(2)}) collective-permute-start(bf16[4,128,1024]{2,1,0:T(8,128)(2,1)S(1)} %broadcast_select_fusion.3), channel_id=1, source_target_pairs={{0,8},{8,0},{4,12},{12,4},{16,24},{24,16},{20,28},{28,20},{1,9},{9... | collective-permute-start | bytes 3145736 | tf_op jit(solution)/shard_map/ppermute | solution.py:22
  84.5 26.1 %collective-permute-start.5 = (bf16[4,128,1024]{2,1,0:T(8,128)(2,1)S(1)}, bf16[4,128,1024]{2,1,0:T(8,128)(2,1)S(1)}, u32[]{:S(2)}, u32[]{:S(2)}) collective-permute-start(bf16[4,128,1024]{2,1,0:T(8,128)(2,1)S(1)} %broadcast_select_fusion.4), channel_id=1, source_target_pairs={{0,16},{16,0},{4,20},{20,4},{8,24},{24,8},{12,28},{28,12},{1,17},{... | collective-permute-start | bytes 3145736 | tf_op jit(solution)/shard_map/ppermute | solution.py:22
  86.6 67.7 %collective-permute-start.2 = (bf16[4,128,2048]{2,1,0:T(8,128)(2,1)S(1)}, bf16[4,128,2048]{2,1,0:T(8,128)(2,1)}, u32[]{:S(2)}, u32[]{:S(2)}) collective-permute-start(bf16[4,128,2048]{2,1,0:T(8,128)(2,1)S(1)} %broadcast_select_fusion.1), channel_id=1, source_target_pairs={{0,16},{16,0},{4,20},{20,4},{8,24},{24,8},{12,28},{28,12},{1,17},{... | collective-permute-start | bytes 6291464 | tf_op jit(solution)/shard_map/ppermute | solution.py:22
  116.7 45.8 %all-to-all-start.1 = ((bf16[512,4,256]{2,0,1:T(8,128)(2,1)}), bf16[512,4,256]{2,0,1:T(8,128)(2,1)}, u32[]{:S(2)}, u32[]{:S(2)}) async-start(bf16[512,4,256]{2,0,1:T(8,128)(2,1)} %copy.27), calls=%async_computation.1 | async-start | bytes 2097152 | tf_op jit(solution)/shard_map/all_to_all | solution.py:116
  162.5 51.9 %all-to-all-start = ((bf16[512,4,512]{2,0,1:T(8,128)(2,1)}), bf16[512,4,512]{2,0,1:T(8,128)(2,1)}, u32[]{:S(2)}, u32[]{:S(2)}) async-start(bf16[512,4,512]{2,0,1:T(8,128)(2,1)} %copy.26), calls=%async_computation | async-start | bytes 4194304 | tf_op jit(solution)/shard_map/all_to_all | solution.py:115
  167.3 0.7 copy-start.1
  167.3 145.8 %all-gather.2.cloned.1.call-start = ((), (), s32[]{:S(2)}) async-start(), calls=%async_computation.3 | async-start | bytes 18874368 | tf_op jit(solution)/shard_map/all_gather | solution.py:122
Sparse Core Ops, SparseCore 0:
  170.0 91.3 all-gather.1
where the time goes:
time: 338 us; the launch traced here: 334 us
  waiting for transfers between devices  168 us (50%)
  blocking collectives  47.4 us (14%)
  local copies, waits for them, and re-layouts  34.7 us (10%)
  matrix products  28.8 us (9%)
  other arithmetic  16.9 us (5%)
  starting transfers between devices  15.6 us (5%)
  between operations  13.5 us (4%)
  loops' own time  8.41 us (2%)
    ppermute x6, waiting for transfers between devices, swapped(): return lax.ppermute(block, axis, route)  127 us
    all_to_all x1, blocking collectives, body(): lax.all_to_all(attended, 'seq', split_axis=0, concat_axis=1, tiled=True)  47.4 us
    all_to_all x1, waiting for transfers between devices, body(): lax.all_to_all(query_tok, 'seq', split_axis=1, concat_axis=0, tiled=True)  40.2 us
    dot_general x1, matrix products, body(): jnp.dot(attended_rows, lax.all_gather(out_weight, 'dp', axis=0, tiled=Tru...  13.9 us
    dot_general x6, matrix products, key_step(): jnp.einsum('cgqk,kcd->qcgd', rounded, value_tile, preferred_element_type=...  9.7 us
    another operation x1, loops' own time, attend_local(): lax.map(per_tile, jnp.arange(seq_rows // tile_rows, dtype=jnp.int32))  7.99 us
  transfers between devices with their start and end apart: 9, of which 5 were waited for; matrix products, arithmetic and copies ran while one was open for 18% of the time, Pallas kernels for 0%

commit v1 on v0

v1 whole, which is shorter than its diff:
```python
import functools
import math

import jax
import jax.numpy as jnp
from jax import lax
from jax.experimental import pallas as pl
from jax.experimental.pallas import tpu as pltpu
from jax.sharding import PartitionSpec as P

HEAD_DIM = 128
BLOCK = 128
VARIANTS = 4


def attend_kernel(blocks, stride, group, table, q_ref, kv_ref, out_ref):
    pair = 2 if group % 2 == 0 else 1
    scale = math.log2(math.e) / math.sqrt(HEAD_DIM)

    def step(t, carry):
        i = t // (group // pair)
        h = t % (group // pair)
        place = table[0, i]
        count = table[1, i]
        variant = (count + stride - 1) // stride
        row = pl.multiple_of(i * BLOCK, BLOCK)
        col = pl.multiple_of(h * pair * HEAD_DIM, pair * HEAD_DIM)
        for v in range(1, VARIANTS + 1):

            @pl.when(variant == v)
            def _(v=v):
                n = v * stride
                first = pl.multiple_of((place - n + 1) * BLOCK, BLOCK)
                q = q_ref[pl.ds(row, BLOCK), pl.ds(col, pair * HEAD_DIM)]
                q = jnp.concatenate(
                    [q[:, a * HEAD_DIM : (a + 1) * HEAD_DIM] for a in range(pair)], axis=0
                )
                k = kv_ref[pl.ds(first, n * BLOCK), :HEAD_DIM]
                val = kv_ref[pl.ds(first, n * BLOCK), HEAD_DIM:]
                s = lax.dot_general(
                    q, k, (((1,), (1,)), ((), ())), preferred_element_type=jnp.float32
                )
                rows = pair * BLOCK
                lead = stride * BLOCK
                at = lax.broadcasted_iota(jnp.int32, (rows, n * BLOCK), 1)
                low = (n - count) * BLOCK
                high = (n - 1) * BLOCK + lax.rem(
                    lax.broadcasted_iota(jnp.int32, (rows, n * BLOCK), 0), BLOCK
                )
                parts = []
                for b in range(n):
                    sl = slice(b * BLOCK, (b + 1) * BLOCK)
                    piece = s[:, sl]
                    if b < stride - 1:
                        piece = jnp.where(at[:, sl] >= low, piece, -jnp.inf)
                    if b == n - 1:
                        piece = jnp.where(at[:, sl] <= high[:, sl], piece, -jnp.inf)
                    parts.append(piece)
                top = functools.reduce(jnp.maximum, parts)
                top = jnp.max(top, axis=1, keepdims=True)
                w = jnp.concatenate(
                    [jnp.exp2((piece - top) * scale).astype(jnp.bfloat16) for piece in parts],
                    axis=1,
                )
                ext = jnp.concatenate([val, jnp.ones_like(val)], axis=1)
                mixed = jnp.dot(w, ext, preferred_element_type=jnp.float32)
                att = (mixed[:, :HEAD_DIM] / mixed[:, HEAD_DIM:]).astype(jnp.bfloat16)
                out_ref[pl.ds(row, BLOCK), pl.ds(col, pair * HEAD_DIM)] = jnp.concatenate(
                    [att[a * BLOCK : (a + 1) * BLOCK] for a in range(pair)], axis=1
                )

        return carry

    lax.fori_loop(0, blocks * (group // pair), step, 0)


def attend(queries, context, table, stride):
    rows, width = queries.shape
    pairs = context.shape[1] // (2 * HEAD_DIM)
    group = width // HEAD_DIM // pairs
    blocks = rows // BLOCK
    return pl.pallas_call(
        functools.partial(attend_kernel, blocks, stride, group),
        grid_spec=pltpu.PrefetchScalarGridSpec(
            num_scalar_prefetch=1,
            grid=(pairs,),
            in_specs=[
                pl.BlockSpec((rows, group * HEAD_DIM), lambda c, t: (0, c)),
                pl.BlockSpec((context.shape[0], 2 * HEAD_DIM), lambda c, t: (0, c)),
            ],
            out_specs=pl.BlockSpec((rows, group * HEAD_DIM), lambda c, t: (0, c)),
        ),
        out_shape=jax.ShapeDtypeStruct((rows, width), jnp.bfloat16),
        compiler_params=pltpu.CompilerParams(vmem_limit_bytes=40 * 1024 * 1024),
        cost_estimate=pl.CostEstimate(
            flops=10**10, bytes_accessed=8 * 10**6, transcendentals=10**6
        ),
        name="attend",
    )(table, queries, context)


def swap_bit(block, marks, bit):
    count = lax.axis_size("dp")
    route = [(g, g ^ (1 << bit)) for g in range(count)]
    partner = lax.ppermute(block, "dp", route)
    moving = (jnp.right_shift(marks, bit) % 2 == 1)[:, None, None]
    return jnp.where(moving, partner, block)


def exchange(block, marks):
    half = block.shape[2] // 2
    bits = list(range(lax.axis_size("dp").bit_length() - 1))
    done = []
    for part, order in ((block[:, :, :half], bits), (block[:, :, half:], bits[:1] + bits[:0:-1])):
        for bit in order:
            part = swap_bit(part, marks, bit)
        done.append(part)
    return jnp.concatenate(done, axis=2)


def body(queries, keys_values, doc_blocks, route_plan, out_weight):
    rows = queries.shape[1]
    blocks = rows // BLOCK
    seq_count = lax.axis_size("seq")
    total_blocks = doc_blocks.shape[1]
    longest = total_blocks // 2
    hops = (longest - 1 + blocks - 1) // blocks
    stride = max(1, longest // VARIANTS)
    marks = route_plan[0]
    own_pairs = exchange(keys_values[0].reshape(blocks, BLOCK, -1), marks).reshape(rows, -1)
    own_queries = exchange(queries[0].reshape(blocks, BLOCK, -1), marks).reshape(rows, -1)
    ring = [(s, s + 1) for s in range(seq_count - 1)]
    context = [own_pairs]
    for _ in range(hops):
        context.insert(0, lax.ppermute(context[0], "seq", ring))
    context = jnp.concatenate(context, axis=0)
    docs = doc_blocks[0]
    own = lax.axis_index("seq") * blocks + jnp.arange(blocks, dtype=jnp.int32)
    own_docs = docs[own]
    start = jnp.sum((docs[None, :] < own_docs[:, None]).astype(jnp.int32), axis=1)
    place = hops * blocks + jnp.arange(blocks, dtype=jnp.int32)
    table = jnp.stack([place, own - start + 1])
    attended = attend(own_queries, context, table, stride)
    layer_out = jnp.dot(
        attended,
        lax.all_gather(out_weight, "dp", axis=0, tiled=True),
        preferred_element_type=jnp.float32,
    )
    return layer_out.astype(jnp.bfloat16)[None]


def solution(mesh):
    in_specs = (
        P("dp", "seq", None),
        P("dp", "seq", None),
        P("dp", None),
        P("seq", None),
        P("dp", None),
    )
    out_specs = P("dp", "seq", None)
    return jax.shard_map(body, mesh=mesh, in_specs=in_specs, out_specs=out_specs, check_vma=False)
```

time: 338 us -> 218 us (0.64)
  the two profiles are of different devices: /device:TPU:0 before, /device:TPU:10 now
where the time goes in v1:
time: 218 us; the launch traced here: 217 us
  waiting for transfers between devices  137 us (63%)
  Pallas kernels  27.6 us (13%)
  starting transfers between devices  18.2 us (8%)
  matrix products  13.7 us (6%)
  between operations  13.5 us (6%)
  other arithmetic  5.25 us (2%)
    ppermute x12, waiting for transfers between devices, swap_bit(): partner = lax.ppermute(block, 'dp', route)  134 us
    pallas_call x1, Pallas kernels, attend(): pl.pallas_call(functools.partial(attend_kernel, blocks, stride, group), g...  27.6 us
    dot_general x1, matrix products, body(): jnp.dot(attended, lax.all_gather(out_weight, 'dp', axis=0, tiled=True), p...  13.7 us
    ppermute x12, starting transfers between devices, swap_bit(): partner = lax.ppermute(block, 'dp', route)  10.9 us
    ppermute x2, starting transfers between devices, body(): context.insert(0, lax.ppermute(context[0], 'seq', ring))  7.27 us
  transfers between devices with their start and end apart: 15, of which 9 were waited for; matrix products, arithmetic and copies ran while one was open for 3% of the time, Pallas kernels for 13%

profile of v1, /device:TPU:10, one launch (start us, length us, event | category | flops | bytes accessed | tf_op | source)
XLA Modules:
  0.0 217.1 jit_solution(12694201877545578605)
XLA Ops:
  6.5 0.7 all-gather.2.cloned.1.call-update
  7.3 0.9 copy-done.1
  8.4 0.5 collective-permute-start.3
  9.1 0.4 collective-permute-start.9
  9.6 3.7 %collective-permute-done.6 = bf16[4,128,512]{2,1,0:T(8,128)(2,1)S(1)} collective-permute-done((bf16[4,128,512]{2,1,0:T(8,128)(2,1)S(1)}, bf16[4,128,512]{2,1,0:T(8,128)(2,1)S(1)}, u32[]{:S(2)}, u32[]{:S(2)}) %collective-permute-start.6) | collective-permute-done | bytes 524320 | tf_op jit(solution)/shard_map/ppermute | solution.py:105
  13.3 0.7 collective-permute-done.9
  14.0 0.2 broadcast_select_fusion.7
  14.2 0.6 collective-permute-start.7
  14.8 1.5 collective-permute-start.10
  16.4 0.5 broadcast_select_fusion.1
  16.8 1.6 collective-permute-start.1
  18.4 18.4 %collective-permute-done.7 = bf16[4,128,512]{2,1,0:T(8,128)(2,1)S(1)} collective-permute-done((bf16[4,128,512]{2,1,0:T(8,128)(2,1)S(1)}, bf16[4,128,512]{2,1,0:T(8,128)(2,1)S(1)}, u32[]{:S(2)}, u32[]{:S(2)}) %collective-permute-start.7) | collective-permute-done | bytes 524320 | tf_op jit(solution)/shard_map/ppermute | solution.py:105
  36.9 1.6 collective-permute-start.8
  38.5 0.5 collective-permute-start.4
  39.0 24.0 %collective-permute-done.8 = bf16[4,128,512]{2,1,0:T(8,128)(2,1)S(1)} collective-permute-done((bf16[4,128,512]{2,1,0:T(8,128)(2,1)S(1)}, bf16[4,128,512]{2,1,0:T(8,128)(2,1)S(1)}, u32[]{:S(2)}, u32[]{:S(2)}) %collective-permute-start.8) | collective-permute-done | bytes 524320 | tf_op jit(solution)/shard_map/ppermute | solution.py:105
  63.2 10.8 %collective-permute-done.1 = bf16[4,128,1024]{2,1,0:T(8,128)(2,1)S(1)} collective-permute-done((bf16[4,128,1024]{2,1,0:T(8,128)(2,1)S(1)}, bf16[4,128,1024]{2,1,0:T(8,128)(2,1)S(1)}, u32[]{:S(2)}, u32[]{:S(2)}) %collective-permute-start.1) | collective-permute-done | bytes 1048608 | tf_op jit(solution)/shard_map/ppermute | solution.py:105
  74.0 0.2 broadcast_select_fusion.3
  74.2 1.6 collective-permute-start.2
  75.8 19.8 %collective-permute-done.11 = bf16[4,128,512]{2,1,0:T(8,128)(2,1)S(1)} collective-permute-done((bf16[4,128,512]{2,1,0:T(8,128)(2,1)S(1)}, bf16[4,128,512]{2,1,0:T(8,128)(2,1)S(1)}, u32[]{:S(2)}, u32[]{:S(2)}) %collective-permute-start.11) | collective-permute-done | bytes 524320 | tf_op jit(solution)/shard_map/ppermute | solution.py:105
  95.9 3.7 %collective-permute-start.12 = (bf16[512,1024]{1,0:T(8,128)(2,1)S(1)}, bf16[512,1024]{1,0:T(8,128)(2,1)}, u32[]{:S(2)}, u32[]{:S(2)}) collective-permute-start(bf16[512,1024]{1,0:T(8,128)(2,1)S(1)} %bitcast.28), channel_id=1, source_target_pairs={{0,1},{1,2},{2,3},{4,5},{5,6},{6,7},{8,9},{9,10},{10,11},{12,13},{... | collective-permute-start | bytes 3145736 | tf_op jit(solution)/shard_map/ppermute | solution.py:135
  99.6 41.1 %collective-permute-done.2 = bf16[4,128,1024]{2,1,0:T(8,128)(2,1)S(1)} collective-permute-done((bf16[4,128,1024]{2,1,0:T(8,128)(2,1)S(1)}, bf16[4,128,1024]{2,1,0:T(8,128)(2,1)S(1)}, u32[]{:S(2)}, u32[]{:S(2)}) %collective-permute-start.2) | collective-permute-done | bytes 1048608 | tf_op jit(solution)/shard_map/ppermute | solution.py:105
  140.6 0.3 broadcast_select_fusion.5
  140.9 2.3 %collective-permute-start.5 = (bf16[4,128,1024]{2,1,0:T(8,128)(2,1)S(1)}, bf16[4,128,1024]{2,1,0:T(8,128)(2,1)}, u32[]{:S(2)}, u32[]{:S(2)}) collective-permute-start(bf16[4,128,1024]{2,1,0:T(8,128)(2,1)S(1)} %get-tuple-element.16), channel_id=1, source_target_pairs={{0,8},{4,12},{8,0},{12,4},{16,24},{20,28},{24,16},{28,20},{1,9},{5... | collective-permute-start | bytes 3145736 | tf_op jit(solution)/shard_map/ppermute | solution.py:105
  143.2 3.6 %collective-permute-start.13 = (bf16[512,1024]{1,0:T(8,128)(2,1)}, bf16[512,1024]{1,0:T(8,128)(2,1)}, u32[]{:S(2)}, u32[]{:S(2)}) collective-permute-start(bf16[512,1024]{1,0:T(8,128)(2,1)} %collective-permute-done.12), channel_id=1, source_target_pairs={{0,1},{1,2},{2,3},{4,5},{5,6},{6,7},{8,9},{9,10},{10,11},{12,13},{... | collective-permute-start | bytes 3145736 | tf_op jit(solution)/shard_map/ppermute | solution.py:135
  146.8 0.6 gather_fusion
  147.5 0.2 convert_reduce_fusion
  147.7 15.9 %collective-permute-done.5 = bf16[4,128,1024]{2,1,0:T(8,128)(2,1)} collective-permute-done((bf16[4,128,1024]{2,1,0:T(8,128)(2,1)S(1)}, bf16[4,128,1024]{2,1,0:T(8,128)(2,1)}, u32[]{:S(2)}, u32[]{:S(2)}) %collective-permute-start.5) | collective-permute-done | bytes 1048608 | tf_op jit(solution)/shard_map/ppermute | solution.py:105
  163.6 1.4 broadcast_select_fusion.2
  165.2 1.9 collective-permute-done.13
  167.1 1.7 pad_maximum_fusion.kv_ref
  168.9 27.6 %attend.1 = bf16[512,2048]{1,0:T(8,128)(2,1)S(1)} custom-call(s32[2,4]{1,0:T(2,128)S(1)} %pad_add_fusion.table, bf16[512,2048]{1,0:T(8,128)(2,1)S(1)} %bitcast.21, bf16[1536,1024]{1,0:T(8,128)(2,1)S(1)} %pad_maximum_fusion.kv_ref), custom_call_target="tpu_custom_call" | custom-call | flops 10000000000 | bytes 8000000 | tf_op jit(solution)/shard_map/attend/pallas_call | solution.py:82
  196.5 13.7 %fusion = bf16[1,512,4096]{2,1,0:T(8,128)(2,1)} fusion(bf16[512,2048]{1,0:T(8,128)(2,1)S(1)} %attend.1, bf16[2048,4096]{1,0:T(8,128)(2,1)} %all-gather.2.cloned.1.call-done), kind=kOutput, calls=%fused_computation.2 | convolution fusion | flops 8592031744 | bytes 23068672 | tf_op jit(solution)/shard_map/dot_general | solution.py:144
  (29 shorter events, 1.4 us)
Async XLA Ops:
  6.5 1.6 copy-start.1
  6.5 2.3 %copy-start.2 = (bf16[1,512,1024]{2,1,0:T(8,128)(2,1)S(1)}, bf16[1,512,1024]{2,1,0:T(8,128)(2,1)}, u32[]{:S(2)}) copy-start(bf16[1,512,1024]{2,1,0:T(8,128)(2,1)} %param.6) | copy-start | bytes 3145732
  6.5 190.0 %all-gather.2.cloned.1.call-start = ((), (), s32[]{:S(2)}) async-start(), calls=%async_computation | async-start | bytes 18874368 | tf_op jit(solution)/shard_map/all_gather | solution.py:146
  8.1 1.4 copy-start.3
  8.3 8.1 %collective-permute-start = (bf16[4,128,1024]{2,1,0:T(8,128)(2,1)S(1)}, bf16[4,128,1024]{2,1,0:T(8,128)(2,1)S(1)}, u32[]{:S(2)}, u32[]{:S(2)}) collective-permute-start(bf16[4,128,1024]{2,1,0:T(8,128)(2,1)S(1)} %get-tuple-element.7), channel_id=1, source_target_pairs={{0,4},{4,0},{8,12},{12,8},{16,20},{20,16},{24,28},{28,24},{1,5},{5... | collective-permute-start | bytes 3145736 | tf_op jit(solution)/shard_map/ppermute | solution.py:105
  8.4 8.0 %collective-permute-start.3 = (bf16[4,128,1024]{2,1,0:T(8,128)(2,1)S(1)}, bf16[4,128,1024]{2,1,0:T(8,128)(2,1)S(1)}, u32[]{:S(2)}, u32[]{:S(2)}) collective-permute-start(bf16[4,128,1024]{2,1,0:T(8,128)(2,1)S(1)} %get-tuple-element.8), channel_id=1, source_target_pairs={{0,4},{4,0},{8,12},{12,8},{16,20},{20,16},{24,28},{28,24},{1,5},{5... | collective-permute-start | bytes 3145736 | tf_op jit(solution)/shard_map/ppermute | solution.py:105
  9.0 4.3 %collective-permute-start.6 = (bf16[4,128,512]{2,1,0:T(8,128)(2,1)S(1)}, bf16[4,128,512]{2,1,0:T(8,128)(2,1)S(1)}, u32[]{:S(2)}, u32[]{:S(2)}) collective-permute-start(bf16[4,128,512]{2,1,0:T(8,128)(2,1)S(1)} %get-tuple-element.11), channel_id=1, source_target_pairs={{0,4},{4,0},{8,12},{12,8},{16,20},{20,16},{24,28},{28,24},{1,5},{5... | collective-permute-start | bytes 1572872 | tf_op jit(solution)/shard_map/ppermute | solution.py:105
  9.1 4.9 %collective-permute-start.9 = (bf16[4,128,512]{2,1,0:T(8,128)(2,1)S(1)}, bf16[4,128,512]{2,1,0:T(8,128)(2,1)S(1)}, u32[]{:S(2)}, u32[]{:S(2)}) collective-permute-start(bf16[4,128,512]{2,1,0:T(8,128)(2,1)S(1)} %get-tuple-element.12), channel_id=1, source_target_pairs={{0,4},{4,0},{8,12},{12,8},{16,20},{20,16},{24,28},{28,24},{1,5},{5... | collective-permute-start | bytes 1572872 | tf_op jit(solution)/shard_map/ppermute | solution.py:105
  14.2 22.5 %collective-permute-start.7 = (bf16[4,128,512]{2,1,0:T(8,128)(2,1)S(1)}, bf16[4,128,512]{2,1,0:T(8,128)(2,1)S(1)}, u32[]{:S(2)}, u32[]{:S(2)}) collective-permute-start(bf16[4,128,512]{2,1,0:T(8,128)(2,1)S(1)} %get-tuple-element.9), channel_id=1, source_target_pairs={{0,8},{4,12},{8,0},{12,4},{16,24},{20,28},{24,16},{28,20},{1,9},{5... | collective-permute-start | bytes 1572872 | tf_op jit(solution)/shard_map/ppermute | solution.py:105
  14.8 24.2 %collective-permute-start.10 = (bf16[4,128,512]{2,1,0:T(8,128)(2,1)S(1)}, bf16[4,128,512]{2,1,0:T(8,128)(2,1)S(1)}, u32[]{:S(2)}, u32[]{:S(2)}) collective-permute-start(bf16[4,128,512]{2,1,0:T(8,128)(2,1)S(1)} %get-tuple-element.10), channel_id=1, source_target_pairs={{0,16},{4,20},{8,24},{12,28},{16,0},{20,4},{24,8},{28,12},{1,17},{... | collective-permute-start | bytes 1572872 | tf_op jit(solution)/shard_map/ppermute | solution.py:105
  16.8 57.2 %collective-permute-start.1 = (bf16[4,128,1024]{2,1,0:T(8,128)(2,1)S(1)}, bf16[4,128,1024]{2,1,0:T(8,128)(2,1)S(1)}, u32[]{:S(2)}, u32[]{:S(2)}) collective-permute-start(bf16[4,128,1024]{2,1,0:T(8,128)(2,1)S(1)} %get-tuple-element.5), channel_id=1, source_target_pairs={{0,8},{4,12},{8,0},{12,4},{16,24},{20,28},{24,16},{28,20},{1,9},{5... | collective-permute-start | bytes 3145736 | tf_op jit(solution)/shard_map/ppermute | solution.py:105
  36.9 26.0 %collective-permute-start.8 = (bf16[4,128,512]{2,1,0:T(8,128)(2,1)S(1)}, bf16[4,128,512]{2,1,0:T(8,128)(2,1)S(1)}, u32[]{:S(2)}, u32[]{:S(2)}) collective-permute-start(bf16[4,128,512]{2,1,0:T(8,128)(2,1)S(1)} %broadcast_select_fusion.9), channel_id=1, source_target_pairs={{0,16},{4,20},{8,24},{12,28},{16,0},{20,4},{24,8},{28,12},{1,17},{... | collective-permute-start | bytes 1572872 | tf_op jit(solution)/shard_map/ppermute | solution.py:105
  38.5 61.0 %collective-permute-start.4 = (bf16[4,128,1024]{2,1,0:T(8,128)(2,1)S(1)}, bf16[4,128,1024]{2,1,0:T(8,128)(2,1)S(1)}, u32[]{:S(2)}, u32[]{:S(2)}) collective-permute-start(bf16[4,128,1024]{2,1,0:T(8,128)(2,1)S(1)} %get-tuple-element.6), channel_id=1, source_target_pairs={{0,16},{4,20},{8,24},{12,28},{16,0},{20,4},{24,8},{28,12},{1,17},{... | collective-permute-start | bytes 3145736 | tf_op jit(solution)/shard_map/ppermute | solution.py:105
  63.1 32.5 %collective-permute-start.11 = (bf16[4,128,512]{2,1,0:T(8,128)(2,1)S(1)}, bf16[4,128,512]{2,1,0:T(8,128)(2,1)S(1)}, u32[]{:S(2)}, u32[]{:S(2)}) collective-permute-start(bf16[4,128,512]{2,1,0:T(8,128)(2,1)S(1)} %get-tuple-element.14), channel_id=1, source_target_pairs={{0,8},{4,12},{8,0},{12,4},{16,24},{20,28},{24,16},{28,20},{1,9},{5... | collective-permute-start | bytes 1572872 | tf_op jit(solution)/shard_map/ppermute | solution.py:105
  74.2 66.4 %collective-permute-start.2 = (bf16[4,128,1024]{2,1,0:T(8,128)(2,1)S(1)}, bf16[4,128,1024]{2,1,0:T(8,128)(2,1)S(1)}, u32[]{:S(2)}, u32[]{:S(2)}) collective-permute-start(bf16[4,128,1024]{2,1,0:T(8,128)(2,1)S(1)} %broadcast_select_fusion.3), channel_id=1, source_target_pairs={{0,16},{4,20},{8,24},{12,28},{16,0},{20,4},{24,8},{28,12},{1,17},{... | collective-permute-start | bytes 3145736 | tf_op jit(solution)/shard_map/ppermute | solution.py:105
  95.8 51.0 %copy-start = (s32[1,16]{1,0:T(1,128)S(1)}, s32[1,16]{1,0:T(1,128)}, u32[]{:S(2)}) copy-start(s32[1,16]{1,0:T(1,128)} %param.7) | copy-start | bytes 196
  95.9 47.4 %collective-permute-start.12 = (bf16[512,1024]{1,0:T(8,128)(2,1)S(1)}, bf16[512,1024]{1,0:T(8,128)(2,1)}, u32[]{:S(2)}, u32[]{:S(2)}) collective-permute-start(bf16[512,1024]{1,0:T(8,128)(2,1)S(1)} %bitcast.28), channel_id=1, source_target_pairs={{0,1},{1,2},{2,3},{4,5},{5,6},{6,7},{8,9},{9,10},{10,11},{12,13},{... | collective-permute-start | bytes 3145736 | tf_op jit(solution)/shard_map/ppermute | solution.py:135
  140.9 22.6 %collective-permute-start.5 = (bf16[4,128,1024]{2,1,0:T(8,128)(2,1)S(1)}, bf16[4,128,1024]{2,1,0:T(8,128)(2,1)}, u32[]{:S(2)}, u32[]{:S(2)}) collective-permute-start(bf16[4,128,1024]{2,1,0:T(8,128)(2,1)S(1)} %get-tuple-element.16), channel_id=1, source_target_pairs={{0,8},{4,12},{8,0},{12,4},{16,24},{20,28},{24,16},{28,20},{1,9},{5... | collective-permute-start | bytes 3145736 | tf_op jit(solution)/shard_map/ppermute | solution.py:105
  143.2 23.9 %collective-permute-start.13 = (bf16[512,1024]{1,0:T(8,128)(2,1)}, bf16[512,1024]{1,0:T(8,128)(2,1)}, u32[]{:S(2)}, u32[]{:S(2)}) collective-permute-start(bf16[512,1024]{1,0:T(8,128)(2,1)} %collective-permute-done.12), channel_id=1, source_target_pairs={{0,1},{1,2},{2,3},{4,5},{5,6},{6,7},{8,9},{9,10},{10,11},{12,13},{... | collective-permute-start | bytes 3145736 | tf_op jit(solution)/shard_map/ppermute | solution.py:135
Sparse Core Ops, SparseCore 0:
  9.2 145.3 all-gather.1

commit v2 on v0

v2 whole, which is shorter than its diff:
```python
import functools
import math

import jax
import jax.numpy as jnp
from jax import lax
from jax.experimental import pallas as pl
from jax.experimental.pallas import tpu as pltpu
from jax.sharding import PartitionSpec as P

HEAD_DIM = 128
BLOCK = 128
MESH = pl.DeviceIdType.MESH


def layer_kernel(
    groups,
    seq_count,
    longest,
    hops,
    doc_ref,
    route_ref,
    q_ref,
    kv_ref,
    w_ref,
    out_ref,
    full_ref,
    q_out,
    q_in,
    kv_out,
    kv_in,
    ctx,
    q_send,
    q_recv,
    kv_send,
    kv_recv,
    w_send,
    w_recv,
    hop_send,
    hop_recv,
    own_sem,
):
    me = lax.axis_index("dp")
    s = lax.axis_index("seq")
    blocks = q_ref.shape[0]
    n_docs = doc_ref.shape[1]
    bit_count = groups.bit_length() - 1
    place = hops * blocks
    bit_of = [lax.rem(lax.div(me, 1 << b), 2) for b in range(bit_count)]

    def partner(offset):
        at = me
        for b in range(bit_count):
            if offset >> b & 1:
                at = at + (1 - 2 * bit_of[b]) * (1 << b)
        return at

    peers = [partner(d) for d in range(groups)]
    right = lax.rem(s + 1, seq_count)
    left = lax.rem(s + seq_count - 1, seq_count)

    barrier = pltpu.get_barrier_semaphore()
    for d in range(1, groups):
        pl.semaphore_signal(barrier, inc=1, device_id={"dp": peers[d]}, device_id_type=MESH)
    for side in (left, right):
        pl.semaphore_signal(barrier, inc=1, device_id={"seq": side}, device_id_type=MESH)

    marks = [route_ref[0, j] for j in range(blocks)]
    taken = []
    for d in range(groups):
        at = jnp.int32(0)
        for j in range(1, blocks):
            at = jnp.where(marks[j] == d, j, at)
        taken.append(at)
    for d in range(1, groups):
        kv_out[d] = kv_ref[taken[d]]
    kv_in[0] = kv_ref[taken[0]]
    pl.semaphore_wait(barrier, groups + 1)

    def slot_copy(src, dst, send, recv, d):
        return pltpu.make_async_remote_copy(
            src_ref=src.at[d],
            dst_ref=dst.at[d],
            send_sem=send.at[d],
            recv_sem=recv.at[d],
            device_id={"dp": peers[d]},
            device_id_type=MESH,
        )

    order = list(range(groups - 1, 0, -1))
    kv_copies = [slot_copy(kv_out, kv_in, kv_send, kv_recv, d) for d in order]
    q_copies = [slot_copy(q_out, q_in, q_send, q_recv, d) for d in order]
    for copy in kv_copies:
        copy.start()
    for d in range(1, groups):
        q_out[d] = q_ref[taken[d]]
    q_in[0] = q_ref[taken[0]]
    for copy in kv_copies:
        copy.wait_send()
    for copy in q_copies:
        copy.start()
    for copy in kv_copies:
        copy.wait_recv()
    for j in range(blocks):
        ctx[pl.ds((place + j) * BLOCK, BLOCK), :] = kv_in[marks[j]]

    for h in range(1, hops + 1):
        skip = place - longest + 1 if h == hops else 0
        rows = (blocks - skip) * BLOCK
        to = ((hops - h) * blocks + skip) * BLOCK
        copy = pltpu.make_async_remote_copy(
            src_ref=ctx.at[pl.ds(to + blocks * BLOCK, rows)],
            dst_ref=ctx.at[pl.ds(to, rows)],
            send_sem=hop_send.at[h - 1],
            recv_sem=hop_recv.at[h - 1],
            device_id={"seq": right},
            device_id_type=MESH,
        )

        @pl.when((s >= h - 1) & (s < seq_count - 1))
        def _(copy=copy):
            copy.start()

        @pl.when(s < h)
        def _(to=to, rows=rows):
            ctx[pl.ds(to, rows), :] = jnp.zeros((rows, ctx.shape[1]), ctx.dtype)

        @pl.when(s >= h)
        def _(copy=copy):
            copy.wait_recv()

        @pl.when((s >= h - 1) & (s < seq_count - 1))
        def _(copy=copy):
            copy.wait_send()

    shard = w_ref.shape[0]
    half_rows = shard // 2
    chip_bits = list(range(1, bit_count))
    paths = (chip_bits, chip_bits[::-1])

    def rows_of(half, offset):
        return pl.ds(pl.multiple_of(peers[offset] * shard + half * half_rows, half_rows), half_rows)

    def piece_copy(half, phase, offset, bit):
        source = w_ref.at[pl.ds(half * half_rows, half_rows)] if offset == 0 else full_ref.at[rows_of(half, offset)]
        return pltpu.make_async_remote_copy(
            src_ref=source,
            dst_ref=full_ref.at[rows_of(half, offset)],
            send_sem=w_send.at[half, phase, offset],
            recv_sem=w_recv.at[half, offset ^ (1 << bit)],
            device_id={"dp": peers[1 << bit]},
            device_id_type=MESH,
        )

    def arrived(half, offset):
        pltpu.make_async_remote_copy(
            src_ref=full_ref.at[rows_of(half, offset)],
            dst_ref=full_ref.at[rows_of(half, offset)],
            send_sem=w_send.at[half, 0, 0],
            recv_sem=w_recv.at[half, offset],
            device_id={"dp": peers[1]},
            device_id_type=MESH,
        ).wait_recv()

    for copy in q_copies[:-2]:
        copy.wait_send()
    sent = []
    own = pltpu.make_async_copy(
        w_ref, full_ref.at[pl.ds(pl.multiple_of(me * shard, shard), shard)], own_sem
    )
    for phase in range(len(chip_bits)):
        for half in range(2):
            sent.append(piece_copy(half, phase, 0, paths[half][phase]))
            sent[-1].start()
    own.start()
    for half in range(2):
        sent.append(piece_copy(half, bit_count - 1, 0, 0))
        sent[-1].start()
    for copy in q_copies[-2:]:
        copy.wait_send()
    for copy in q_copies:
        copy.wait_recv()

    pairs = kv_ref.shape[2] // (2 * HEAD_DIM)
    group = q_ref.shape[2] // HEAD_DIM // pairs
    wide = 2 if group % 2 == 0 else 1
    scale = math.log2(math.e) / math.sqrt(HEAD_DIM)
    per_pair = group // wide

    def attend(t, carry):
        i = lax.div(t, pairs * per_pair)
        u = lax.rem(t, pairs * per_pair)
        c = lax.div(u, per_pair)
        mine = s * blocks + i
        doc = doc_ref[0, mine]
        start = jnp.int32(0)
        for b in range(n_docs):
            start = start + jnp.where(doc_ref[0, b] < doc, 1, 0)
        low = (longest - 1 - mine + start) * BLOCK
        col = pl.multiple_of(u * wide * HEAD_DIM, wide * HEAD_DIM)
        q = q_in[route_ref[0, i], :, pl.ds(col, wide * HEAD_DIM)]
        q = jnp.concatenate(
            [q[:, a * HEAD_DIM : (a + 1) * HEAD_DIM] for a in range(wide)], axis=0
        )
        first = pl.multiple_of((place + 1 - longest + i) * BLOCK, BLOCK)
        kcol = pl.multiple_of(c * 2 * HEAD_DIM, 2 * HEAD_DIM)
        window = ctx[pl.ds(first, longest * BLOCK), pl.ds(kcol, 2 * HEAD_DIM)]
        k = window[:, :HEAD_DIM]
        val = window[:, HEAD_DIM:]
        scores = lax.dot_general(
            q, k, (((1,), (1,)), ((), ())), preferred_element_type=jnp.float32
        )
        rows = wide * BLOCK
        column = lax.broadcasted_iota(jnp.int32, (rows, BLOCK), 1)
        row = lax.rem(lax.broadcasted_iota(jnp.int32, (rows, BLOCK), 0), BLOCK)
        parts = []
        for b in range(longest):
            piece = scores[:, b * BLOCK : (b + 1) * BLOCK]
            if b < longest - 1:
                piece = jnp.where(column >= low - b * BLOCK, piece, -jnp.inf)
            else:
                piece = jnp.where(column <= row, piece, -jnp.inf)
            parts.append(piece)
        top = jnp.max(functools.reduce(jnp.maximum, parts), axis=1, keepdims=True)
        weights = jnp.concatenate(
            [jnp.exp2((piece - top) * scale).astype(jnp.bfloat16) for piece in parts], axis=1
        )
        mixed = jnp.dot(
            weights,
            jnp.concatenate([val, jnp.ones_like(val)], axis=1),
            preferred_element_type=jnp.float32,
        )
        att = (mixed[:, :HEAD_DIM] / mixed[:, HEAD_DIM:]).astype(jnp.bfloat16)
        out_ref[pl.ds(pl.multiple_of(i * BLOCK, BLOCK), BLOCK), pl.ds(col, wide * HEAD_DIM)] = (
            jnp.concatenate([att[a * BLOCK : (a + 1) * BLOCK] for a in range(wide)], axis=1)
        )
        return carry

    lax.fori_loop(0, blocks * pairs * per_pair, attend, 0)

    seen = set()

    def need(half, offset):
        if (half, offset) not in seen:
            seen.add((half, offset))
            arrived(half, offset)

    held = [[0], [0]]
    for phase in range(len(chip_bits)):
        for half in range(2):
            bit = paths[half][phase]
            for offset in held[half]:
                if offset:
                    need(half, offset)
                    sent.append(piece_copy(half, phase, offset, bit))
                    sent[-1].start()
            held[half] = held[half] + [o ^ (1 << bit) for o in held[half]]
    for place_in in range(1, len(held[0])):
        for half in range(2):
            offset = held[half][place_in]
            need(half, offset)
            sent.append(piece_copy(half, bit_count - 1, offset, 0))
            sent[-1].start()
    for half in range(2):
        for offset in range(1, groups, 2):
            need(half, offset)
    own.wait()
    for copy in sent:
        copy.wait_send()


def body(queries, keys_values, doc_blocks, route_plan, out_weight):
    rows, width = queries.shape[1:]
    pair_width = keys_values.shape[2]
    blocks = rows // BLOCK
    seq_count = lax.axis_size("seq")
    groups = lax.axis_size("dp")
    bit_count = groups.bit_length() - 1
    longest = doc_blocks.shape[1] // 2
    hops = (longest - 1 + blocks - 1) // blocks
    dtype = queries.dtype
    vmem = pl.BlockSpec(memory_space=pltpu.VMEM)
    smem = pl.BlockSpec(memory_space=pltpu.SMEM)
    anyspace = pl.BlockSpec(memory_space=pl.ANY)
    dma = pltpu.SemaphoreType.DMA
    attended, weight = pl.pallas_call(
        functools.partial(layer_kernel, groups, seq_count, longest, hops),
        in_specs=[smem, smem, vmem, vmem, anyspace],
        out_specs=[vmem, anyspace],
        out_shape=[
            jax.ShapeDtypeStruct((rows, width), dtype),
            jax.ShapeDtypeStruct((out_weight.shape[0] * groups, out_weight.shape[1]), dtype),
        ],
        scratch_shapes=[
            pltpu.VMEM((groups, BLOCK, width), dtype),
            pltpu.VMEM((groups, BLOCK, width), dtype),
            pltpu.VMEM((groups, BLOCK, pair_width), dtype),
            pltpu.VMEM((groups, BLOCK, pair_width), dtype),
            pltpu.VMEM(((hops + 1) * rows, pair_width), dtype),
            dma((groups,)),
            dma((groups,)),
            dma((groups,)),
            dma((groups,)),
            dma((2, bit_count, groups)),
            dma((2, groups)),
            dma((hops,)),
            dma((hops,)),
            dma,
        ],
        compiler_params=pltpu.CompilerParams(
            collective_id=0, has_side_effects=True, vmem_limit_bytes=52 * 1024 * 1024
        ),
        cost_estimate=pl.CostEstimate(
            flops=10**10, bytes_accessed=3 * 10**7, transcendentals=10**7
        ),
        name="layer",
    )(
        doc_blocks,
        route_plan,
        queries[0].reshape(blocks, BLOCK, width),
        keys_values[0].reshape(blocks, BLOCK, pair_width),
        out_weight,
    )
    layer_out = jnp.dot(attended, weight, preferred_element_type=jnp.float32)
    return layer_out.astype(jnp.bfloat16)[None]


def solution(mesh):
    in_specs = (
        P("dp", "seq", None),
        P("dp", "seq", None),
        P("dp", None),
        P("seq", None),
        P("dp", None),
    )
    out_specs = P("dp", "seq", None)
    return jax.shard_map(body, mesh=mesh, in_specs=in_specs, out_specs=out_specs, check_vma=False)
```

time: 338 us -> 167 us (0.49); the launches traced: 334 us -> 167 us
  waiting for transfers between devices: 168 us -> 0 us
  Pallas kernels: 0 us -> 150 us
  blocking collectives: 47.4 us -> 0 us
  local copies, waits for them, and re-layouts: 34.7 us -> 2.53 us
  other arithmetic: 16.9 us -> 0 us
  starting transfers between devices: 15.6 us -> 0 us
  matrix products: 28.8 us -> 14.3 us
  between operations: 13.5 us -> 0.01 us
  loops' own time: 8.41 us -> 0 us
    pallas_call x0 -> x1, Pallas kernels: none -> 150 us  [body(): pl.pallas_call(functools.partial(layer_kernel, groups, seq_count, longest...]
    ppermute x6 -> x0, waiting for transfers between devices: 127 us -> none  [swapped(): return lax.ppermute(block, axis, route)]
    all_to_all x1 -> x0, blocking collectives: 47.4 us -> none  [body(): lax.all_to_all(attended, 'seq', split_axis=0, concat_axis=1, tiled=True)]
    all_to_all x2 -> x0, waiting for transfers between devices: 40.2 us -> none  [the longest x1 40.2 us: body(): lax.all_to_all(query_tok, 'seq', split_axis=1, concat_axis=0, tiled=True)]
    dot_general x13 -> x1, matrix products: 28.8 us -> 14.3 us  [body(): layer_out = jnp.dot(attended, weight, preferred_element_type=jnp.float32)]
    dynamic_slice x26 -> x0, local copies, waits for them, and re-layouts: 10.7 us -> none  [the longest x8 5.17 us: per_tile(): query_tile = lax.dynamic_slice_in_dim(query_view, first_row, tile_rows, 0)]
    all_to_all x4 -> x0, local copies, waits for them, and re-layouts: 10 us -> none  [the longest x2 5.04 us: body(): lax.all_to_all(query_tok, 'seq', split_axis=1, concat_axis=0, tiled=True)]
    all_to_all x2 -> x0, starting transfers between devices: 9.94 us -> none  [the longest x1 5.14 us: body(): lax.all_to_all(pair_wide, 'seq', split_axis=1, concat_axis=0, tiled=True)]
  transfers between devices with their start and end apart: 9 -> 0, of which waited for: 5 -> 0; matrix products, arithmetic and copies ran while one was open for 18% -> 0% of each run, Pallas kernels for 0% -> 0%
where the time goes in v2:
time: 167 us
  Pallas kernels  150 us (90%)
  matrix products  14.3 us (9%)
  local copies, waits for them, and re-layouts  2.53 us (2%)
    pallas_call x1, Pallas kernels, body(): pl.pallas_call(functools.partial(layer_kernel, groups, seq_count, longest...  150 us
    dot_general x1, matrix products, body(): layer_out = jnp.dot(attended, weight, preferred_element_type=jnp.float32)  14.3 us

profile of v2, /device:TPU:0, one launch (start us, length us, event | category | flops | bytes accessed | tf_op | source)
XLA Modules:
  0.0 166.8 jit_solution(7831902681102199441)
XLA Ops:
  0.0 0.0 copy-start
  0.0 1.2 copy-done
  1.2 0.0 copy-start.1
  1.2 0.7 copy-done.1
  1.9 0.0 copy-start.2
  1.9 0.7 copy-done.2
  2.5 150.0 %layer.1 = (bf16[512,2048]{1,0:T(8,128)(2,1)}, bf16[2048,4096]{1,0:T(8,128)(2,1)}) custom-call(s32[1,16]{1,0:T(1,128)S(1)} %copy-done.1, s32[1,4]{1,0:T(1,128)S(1)} %copy-done.2, bf16[4,128,2048]{2,1,0:T(8,128)(2,1)} %bitcast.7, bf16[4,128,1024]{2,1,0:T(8,128)(2,1)S(1)} %bitcast.6, bf16[256,4096]{1,0:T(8,128)(2,1)} %w_ref.1), custom_call_target="tpu_custom_call" | custom-call | flops 10000000000 | bytes 30000000 | tf_op jit(solution)/shard_map/layer/pallas_call | solution.py:286
  152.5 14.3 %fusion = bf16[1,512,4096]{2,1,0:T(8,128)(2,1)} fusion(bf16[512,2048]{1,0:T(8,128)(2,1)} %get-tuple-element.7, bf16[2048,4096]{1,0:T(8,128)(2,1)} %get-tuple-element.8), kind=kOutput, calls=%fused_computation.1 | convolution fusion | flops 8592031744 | bytes 23068672 | tf_op jit(solution)/shard_map/dot_general | solution.py:324
Async XLA Ops:
  0.0 1.2 copy-start
  1.2 0.7 copy-start.1
  1.9 0.7 copy-start.2

commit v3 on v2

--- a/solution.py
+++ b/solution.py
@@ -10,6 +10,7 @@
 
 HEAD_DIM = 128
 BLOCK = 128
+PARTS = 4
 MESH = pl.DeviceIdType.MESH
 
 
@@ -95,14 +96,42 @@
     for d in range(1, groups):
         q_out[d] = q_ref[taken[d]]
     q_in[0] = q_ref[taken[0]]
-    for copy in kv_copies:
-        copy.wait_send()
-    for copy in q_copies:
+    for at, copy in enumerate(q_copies):
+        kv_copies[at].wait_send()
         copy.start()
     for copy in kv_copies:
         copy.wait_recv()
     for j in range(blocks):
         ctx[pl.ds((place + j) * BLOCK, BLOCK), :] = kv_in[marks[j]]
+
+    shard = w_ref.shape[0]
+    half_rows = shard // PARTS
+    chip_bits = list(range(1, bit_count))
+    paths = [chip_bits, chip_bits[::-1]] * (PARTS // 2)
+
+    def rows_of(half, offset):
+        return pl.ds(pl.multiple_of(peers[offset] * shard + half * half_rows, half_rows), half_rows)
+
+    def piece_copy(half, phase, offset, bit):
+        source = w_ref.at[pl.ds(half * half_rows, half_rows)] if offset == 0 else full_ref.at[rows_of(half, offset)]
+        return pltpu.make_async_remote_copy(
+            src_ref=source,
+            dst_ref=full_ref.at[rows_of(half, offset)],
+            send_sem=w_send.at[half, phase, offset],
+            recv_sem=w_recv.at[half, offset ^ (1 << bit)],
+            device_id={"dp": peers[1 << bit]},
+            device_id_type=MESH,
+        )
+
+    def arrived(half, offset):
+        pltpu.make_async_remote_copy(
+            src_ref=full_ref.at[rows_of(half, offset)],
+            dst_ref=full_ref.at[rows_of(half, offset)],
+            send_sem=w_send.at[half, 0, 0],
+            recv_sem=w_recv.at[half, offset],
+            device_id={"dp": peers[1]},
+            device_id_type=MESH,
+        ).wait_recv()
 
     for h in range(1, hops + 1):
         skip = place - longest + 1 if h == hops else 0
@@ -125,6 +154,22 @@
         def _(to=to, rows=rows):
             ctx[pl.ds(to, rows), :] = jnp.zeros((rows, ctx.shape[1]), ctx.dtype)
 
+        if h == hops:
+            for first_copy in q_copies[:-2]:
+                first_copy.wait_send()
+            sent = []
+            own = pltpu.make_async_copy(
+                w_ref, full_ref.at[pl.ds(pl.multiple_of(me * shard, shard), shard)], own_sem
+            )
+            for phase in range(len(chip_bits)):
+                for half in range(PARTS):
+                    sent.append(piece_copy(half, phase, 0, paths[half][phase]))
+                    sent[-1].start()
+            own.start()
+            for half in range(PARTS):
+                sent.append(piece_copy(half, bit_count - 1, 0, 0))
+                sent[-1].start()
+
         @pl.when(s >= h)
         def _(copy=copy):
             copy.wait_recv()
@@ -133,49 +178,6 @@
         def _(copy=copy):
             copy.wait_send()
 
-    shard = w_ref.shape[0]
-    half_rows = shard // 2
-    chip_bits = list(range(1, bit_count))
-    paths = (chip_bits, chip_bits[::-1])
-
-    def rows_of(half, offset):
-        return pl.ds(pl.multiple_of(peers[offset] * shard + half * half_rows, half_rows), half_rows)
-
-    def piece_copy(half, phase, offset, bit):
-        source = w_ref.at[pl.ds(half * half_rows, half_rows)] if offset == 0 else full_ref.at[rows_of(half, offset)]
-        return pltpu.make_async_remote_copy(
-            src_ref=source,
-            dst_ref=full_ref.at[rows_of(half, offset)],
-            send_sem=w_send.at[half, phase, offset],
-            recv_sem=w_recv.at[half, offset ^ (1 << bit)],
-            device_id={"dp": peers[1 << bit]},
-            device_id_type=MESH,
-        )
-
-    def arrived(half, offset):
-        pltpu.make_async_remote_copy(
-            src_ref=full_ref.at[rows_of(half, offset)],
-            dst_ref=full_ref.at[rows_of(half, offset)],
-            send_sem=w_send.at[half, 0, 0],
-            recv_sem=w_recv.at[half, offset],
-            device_id={"dp": peers[1]},
-            device_id_type=MESH,
-        ).wait_recv()
-
-    for copy in q_copies[:-2]:
-        copy.wait_send()
-    sent = []
-    own = pltpu.make_async_copy(
-        w_ref, full_ref.at[pl.ds(pl.multiple_of(me * shard, shard), shard)], own_sem
-    )
-    for phase in range(len(chip_bits)):
-        for half in range(2):
-            sent.append(piece_copy(half, phase, 0, paths[half][phase]))
-            sent[-1].start()
-    own.start()
-    for half in range(2):
-        sent.append(piece_copy(half, bit_count - 1, 0, 0))
-        sent[-1].start()
     for copy in q_copies[-2:]:
         copy.wait_send()
     for copy in q_copies:
@@ -236,7 +238,8 @@
         )
         return carry
 
-    lax.fori_loop(0, blocks * pairs * per_pair, attend, 0)
+    steps = blocks * pairs * per_pair
+    lax.fori_loop(0, steps // 2, attend, 0)
 
     seen = set()
 
@@ -245,9 +248,9 @@
             seen.add((half, offset))
             arrived(half, offset)
 
-    held = [[0], [0]]
+    held = [[0] for _ in range(PARTS)]
     for phase in range(len(chip_bits)):
-        for half in range(2):
+        for half in range(PARTS):
             bit = paths[half][phase]
             for offset in held[half]:
                 if offset:
@@ -255,13 +258,14 @@
                     sent.append(piece_copy(half, phase, offset, bit))
                     sent[-1].start()
             held[half] = held[half] + [o ^ (1 << bit) for o in held[half]]
+    lax.fori_loop(steps // 2, steps, attend, 0)
     for place_in in range(1, len(held[0])):
-        for half in range(2):
+        for half in range(PARTS):
             offset = held[half][place_in]
             need(half, offset)
             sent.append(piece_copy(half, bit_count - 1, offset, 0))
             sent[-1].start()
-    for half in range(2):
+    for half in range(PARTS):
         for offset in range(1, groups, 2):
             need(half, offset)
     own.wait()
@@ -301,8 +305,8 @@
             dma((groups,)),
             dma((groups,)),
             dma((groups,)),
-            dma((2, bit_count, groups)),
-            dma((2, groups)),
+            dma((PARTS, bit_count, groups)),
+            dma((PARTS, groups)),
             dma((hops,)),
             dma((hops,)),
             dma,

time: 167 us -> 166 us (level)
  no operation moved by 1% of the time
where the time goes in v3:
time: 166 us
  Pallas kernels  149 us (90%)
  matrix products  14.3 us (9%)
  local copies, waits for them, and re-layouts  2.53 us (2%)
    pallas_call x1, Pallas kernels, body(): pl.pallas_call(functools.partial(layer_kernel, groups, seq_count, longest...  149 us
    dot_general x1, matrix products, body(): layer_out = jnp.dot(attended, weight, preferred_element_type=jnp.float32)  14.3 us

profile of v3, /device:TPU:0, one launch (start us, length us, event | category | flops | bytes accessed | tf_op | source)
XLA Modules:
  0.0 165.9 jit_solution(17289231042742206257)
XLA Ops:
  0.0 0.0 copy-start
  0.0 1.2 copy-done
  1.2 0.0 copy-start.1
  1.2 0.7 copy-done.1
  1.9 0.0 copy-start.2
  1.9 0.7 copy-done.2
  2.5 149.0 %layer.1 = (bf16[512,2048]{1,0:T(8,128)(2,1)}, bf16[2048,4096]{1,0:T(8,128)(2,1)}) custom-call(s32[1,16]{1,0:T(1,128)S(1)} %copy-done.1, s32[1,4]{1,0:T(1,128)S(1)} %copy-done.2, bf16[4,128,2048]{2,1,0:T(8,128)(2,1)} %bitcast.7, bf16[4,128,1024]{2,1,0:T(8,128)(2,1)S(1)} %bitcast.6, bf16[256,4096]{1,0:T(8,128)(2,1)} %w_ref.1), custom_call_target="tpu_custom_call" | custom-call | flops 10000000000 | bytes 30000000 | tf_op jit(solution)/shard_map/layer/pallas_call | solution.py:290
  151.6 14.3 %fusion = bf16[1,512,4096]{2,1,0:T(8,128)(2,1)} fusion(bf16[512,2048]{1,0:T(8,128)(2,1)} %get-tuple-element.7, bf16[2048,4096]{1,0:T(8,128)(2,1)} %get-tuple-element.8), kind=kOutput, calls=%fused_computation.1 | convolution fusion | flops 8592031744 | bytes 23068672 | tf_op jit(solution)/shard_map/dot_general | solution.py:328
Async XLA Ops:
  0.0 1.2 copy-start
  1.2 0.7 copy-start.1
  1.9 0.7 copy-start.2
